TPU v7x, 32 devices: a whole 2x2x4 slice. The times are simulated.
32 devices in a mesh: gr: 4 (over y, core), gc: 8 (over z, x).
Axes of the slice: x: 2, y: 2, z: 4, core: 2. Of those that a mesh axis runs over, the one named last changes fastest.
Arguments:
- features: bfloat16 [4096, 1024], P(('gr', 'gc')), may hold values from -6 to 6
- weight: bfloat16 [1024, 1024], replicated, may hold values from -0.1875 to 0.1875
- cotangent: bfloat16 [4096, 1024], P(('gr', 'gc')), may hold values from -6 to 6
- block_values: bfloat16 [32, 4, 128, 128], P(('gr', 'gc')), as said below
- block_codes: int32 [32, 4], P(('gr', 'gc')), may hold values from 0 to 31, as said below
- block_count: int32 [32], P(('gr', 'gc')), may hold values from 1 to 4, as said below
Outputs:
- output: float32 [4096, 1024], P(('gr', 'gc'))
- input_grad: float32 [4096, 1024], P(('gr', 'gc'))
- weight_grad: float32 [1024, 1024], P('gc')
Inputs may be any that keep to these rules, and one draw needn't show every extreme that they name: `block_codes`: write code = row * 32 + column. In every slot, row lies in 0 to 0 and column is a block of a slice s + j * 8 with |j| <= 2 (same grid column, at most 2 grid rows away). The codes of the live slots of one slice differ from one another. Every diagonal block (block row equal to block column) is live. The live slots of a slice are its first block_count slots; the entries of later slots are not part of the adjacency. In every draw some slice has all 4 slots live. `block_values`: the adjacency is symmetric: a block is live exactly when its mirror block is, and its entries are the transpose of the mirror's.
All inputs are finite; a program needn't handle non-finite values.
Results may differ from a plain program's by a relative error of at most 0.0045.
Values may be sent and summed in bfloat16 or wider, within the bound.
A program may use at most 64 MiB of HBM per device.

v0:
```python
import functools

import jax
import jax.numpy as jnp
from jax import lax
from jax.experimental import pallas as pl
from jax.experimental.pallas import tpu as pltpu
from jax.sharding import PartitionSpec as P

MESH = pl.DeviceIdType.MESH
GRANT = 62 * 1024 * 1024


def dense_tile(row_index, block_index, active, values, piece_blocks, row_blocks):
    block_size = values.shape[-1]
    select_col = (block_index[:, None] == jnp.arange(piece_blocks)[None, :]) & active[:, None]
    select_row = row_index[:, None] == jnp.arange(row_blocks)[None, :]
    tiled = jnp.einsum(
        "ka,km,kij->aimj",
        select_row.astype(jnp.bfloat16),
        select_col.astype(jnp.bfloat16),
        values,
        preferred_element_type=jnp.float32,
    )
    return tiled.astype(jnp.bfloat16).reshape(row_blocks * block_size, piece_blocks * block_size)


def aggregate(source, layout):
    row_index, block_index, active, values = layout
    node_rows = source.shape[0]
    block_size = values.shape[-1]
    row_blocks = node_rows // block_size
    portion = lax.all_gather(source, "gr", axis=0, tiled=True)
    tile = dense_tile(
        row_index, block_index, active, values, portion.shape[0] // block_size, row_blocks
    )
    return jnp.dot(tile, portion, preferred_element_type=jnp.float32)


def by_rows(features, weight, cotangent, block_values, block_codes, block_count):
    node_rows = features.shape[0]
    block_size = block_values.shape[-1]
    row_blocks = node_rows // block_size
    grid_cols = lax.axis_size("gc")
    grid_rows = lax.axis_size("gr")
    all_blocks = row_blocks * grid_rows * grid_cols
    slot_codes = block_codes[0]
    row_index = slot_codes // all_blocks
    column_block = slot_codes % all_blocks
    block_index = column_block // row_blocks // grid_cols * row_blocks + column_block % row_blocks
    active = jnp.arange(slot_codes.shape[0]) < block_count[0]
    layout = (row_index, block_index, active, block_values[0])
    projected = jnp.dot(features, weight, preferred_element_type=jnp.float32).astype(jnp.bfloat16)
    summed = aggregate(projected, layout)
    sigmoid = jax.nn.sigmoid(summed)
    output = summed * sigmoid
    act_slope = (cotangent.astype(jnp.float32) * sigmoid * (1.0 + summed * (1.0 - sigmoid))).astype(
        jnp.bfloat16
    )
    back_grad = aggregate(act_slope, layout).astype(jnp.bfloat16)
    input_grad = lax.dot_general(
        back_grad, weight, (((1,), (1,)), ((), ())), preferred_element_type=jnp.float32
    )
    grad_scale = (node_rows * grid_rows * grid_cols) ** (-0.5)
    partial_grad = (
        lax.dot_general(
            features, back_grad, (((0,), (0,)), ((), ())), preferred_element_type=jnp.float32
        )
        * grad_scale
    )
    row_share = lax.psum_scatter(partial_grad, "gc", scatter_dimension=0, tiled=True)
    weight_grad = lax.psum(row_share, "gr")
    return (output, input_grad, weight_grad)


def layer_kernel(
    n_gr, n_gc, scale,
    feat, wt, cot, vals, codes, count,
    out_o, ig_o, wg_o,
    fa, ft, wq, wv, vv, aa, pj, cq, sl, ob, bq, br, iv, xs, xr, ac, wa,
    loc, f_s, f_r, g_s, g_r, a_s, a_r, b_s, b_r, w_s, w_r, v_s, v_r,
    c_s, c_r, o_s, o_r, k_s, k_r, x_s, x_r,
):
    rows, width = feat.shape
    share = width // n_gr
    chips = n_gr // 2
    r, g = lax.axis_index("gr"), lax.axis_index("gc")
    chip, core = r // 2, r % 2
    mate = chip * 2 + 1 - core
    f32, bf16 = jnp.float32, jnp.bfloat16

    def rowsof(s):
        return pl.ds(pl.multiple_of(s * rows, rows), rows)

    def cols(s):
        return pl.ds(pl.multiple_of(s * share, share), share)

    def flip(at, m):
        for bit in (1 << b for b in range(n_gc.bit_length())):
            if m & bit:
                at = at + bit - 2 * bit * (at // bit % 2)
        return at

    def send(src, dst, ss, rs, where):
        copy = pltpu.make_async_remote_copy(
            src_ref=src, dst_ref=dst, send_sem=ss, recv_sem=rs, device_id=where,
            device_id_type=MESH,
        )
        copy.start()
        return copy

    def peer(j):
        return lax.rem(r + j, n_gr)

    local_w = pltpu.make_async_copy(wt.at[:, cols(r)], wq, loc.at[0])
    local_f = pltpu.make_async_copy(feat, fa.at[r], loc.at[1])
    local_v = pltpu.make_async_copy(vals.at[0], vv, loc.at[2])
    local_c = pltpu.make_async_copy(cot.at[:, cols(r)], cq.at[r], loc.at[3])
    local_all = pltpu.make_async_copy(wt, wv, loc.at[4])
    for copy in (local_v, local_f, local_w, local_c, local_all):
        copy.start()

    barrier = pltpu.get_barrier_semaphore()
    for j in range(1, n_gr):
        pl.semaphore_signal(barrier, inc=1, device_id={"gr": peer(j)}, device_id_type=MESH)
    bits = [1 << b for b in range(n_gc.bit_length() - 1)]
    for bit in bits:
        pl.semaphore_signal(barrier, inc=1, device_id={"gc": flip(g, bit)}, device_id_type=MESH)
    pl.semaphore_wait(barrier, n_gr - 1 + len(bits))

    far = range(1, chips)
    half = rows // 2
    halves = (pl.ds(0, half), pl.ds(half, half))

    def ahead(d):
        return lax.rem(chip + d, chips) * 2 + core

    def behind(d):
        return lax.rem(chip + chips - d, chips) * 2 + core

    f_far = {
        (d, h): send(
            feat.at[part, :], fa.at[r, part, :], f_s.at[d, h], f_r.at[d, h], {"gr": ahead(d)}
        )
        for h, part in enumerate(halves)
        for d in far
    }
    f_mate = send(feat, fa.at[r], f_s.at[0, 0], f_r.at[0, 0], {"gr": mate})

    local_v.wait()
    for m in range(n_gr):
        tile = jnp.zeros((rows, rows), f32)
        for k in range(vv.shape[0]):
            hit = jnp.logical_and(k < count[0], (codes[0, k] % (n_gr * n_gc)) // n_gc == m)
            tile = tile + vv[k].astype(f32) * jnp.where(hit, 1.0, 0.0)
        aa[rowsof(r), m * rows:(m + 1) * rows] = tile.astype(bf16)

    def listed(s):
        if chips == 2:
            pair = pl.ds(pl.multiple_of(s // 2 * (2 * rows), 2 * rows), 2 * rows)
            return aa.at[rowsof(s), pair]
        return aa.at[rowsof(s), :]

    a_far = [send(listed(r), listed(r), a_s.at[d], a_r.at[d], {"gr": ahead(d)}) for d in far]
    a_mate = send(aa.at[rowsof(r)], aa.at[rowsof(r)], a_s.at[0], a_r.at[0], {"gr": mate})

    def project(s):
        pj[rowsof(s), :] = jnp.dot(fa[s], wq[...], preferred_element_type=f32).astype(bf16)

    def turn(s):
        ft[:, rowsof(s)] = fa[s].T

    local_f.wait()
    local_w.wait()
    project(r)
    turn(r)
    f_mate.wait_recv()
    project(mate)
    turn(mate)

    f_next = {}
    c_all = []
    for h, part in enumerate(halves):
        for d in far:
            f_far[d, h].wait_recv()
            here = fa.at[behind(d), part, :]
            f_next[d, h] = send(here, here, g_s.at[d, h], g_r.at[d, h], {"gr": mate})
        if h == 0:
            c_all = [
                send(cot.at[:, cols(peer(j))], cq.at[r], c_s.at[j], c_r.at[j], {"gr": peer(j)})
                for j in range(1, n_gr)
            ]
    a_next = []
    for d in far:
        a_far[d - 1].wait_recv()
        here = listed(behind(d))
        a_next.append(send(here, here, b_s.at[d], b_r.at[d], {"gr": mate}))
    for d in far:
        project(behind(d))
    a_mate.wait_recv()
    if chips == 2:
        for t in (r, mate):
            for s in (lax.rem(chip + 1, 2) * 2, lax.rem(chip + 1, 2) * 2 + 1):
                aa[rowsof(s), rowsof(t)] = aa[rowsof(t), rowsof(s)].T
    for d in far:
        for h in range(2):
            f_next[d, h].wait_recv()
        project(behind(d) + 1 - 2 * core)
    for copy in a_next:
        copy.wait_recv()

    for i in range(n_gr):
        summed = jnp.dot(aa[i * rows:(i + 1) * rows, :], pj[...], preferred_element_type=f32)
        sigmoid = jax.nn.sigmoid(summed)
        ob[i] = (summed * sigmoid).astype(bf16)
        sl[i] = sigmoid * (1.0 + summed * (1.0 - sigmoid))
    for d in far:
        turn(behind(d))
        turn(behind(d) + 1 - 2 * core)
    local_c.wait()
    for copy in c_all:
        copy.wait_recv()
    slope_all = (cq[...].astype(f32) * sl[...]).astype(bf16).reshape(n_gr * rows, share)
    for i in range(n_gr):
        bq[i] = jnp.dot(
            aa[i * rows:(i + 1) * rows, :], slope_all, preferred_element_type=f32
        ).astype(bf16)
    back = bq[...].reshape(n_gr * rows, share)

    depth, part = width // n_gc, share // 2
    sides = [bits, bits[1::-1] + bits[2:]]
    x_all = {}

    def push(h, m, bit, value):
        xs[h, m] = value.astype(bf16)
        x_all[h, m] = send(
            xs.at[h, m], xr.at[h, m], x_s.at[h, m], x_r.at[h, m], {"gc": flip(g, bit)}
        )

    def grad_rows(m):
        at = pl.ds(pl.multiple_of(flip(g, m) * depth, depth), depth)
        ac[m] = jnp.dot(ft[at, :], back, preferred_element_type=f32)

    def gathered(h, m):
        total = ac[m, :, h * part:(h + 1) * part]
        for bit in sides[h]:
            if m & bit:
                break
            x_all[h, m + bit].wait_recv()
            total = total + xr[h, m + bit].astype(f32)
        return total

    def rank(h, m):
        return sum(1 << t for t, bit in enumerate(sides[h]) if m & bit)

    firsts = [order[0] for order in sides]
    for m in range(n_gc - 1, 0, -1):
        if any(m & bit for bit in firsts):
            grad_rows(m)
            for h, bit in enumerate(firsts):
                if m & bit:
                    push(h, m, bit, ac[m, :, h * part:(h + 1) * part])
    k_all = [
        send(bq.at[peer(j)], br.at[:, cols(r)], k_s.at[j], k_r.at[j], {"gr": peer(j)})
        for j in range(1, n_gr)
    ]
    o_all = [
        send(ob.at[peer(j)], out_o.at[:, cols(r)], o_s.at[j], o_r.at[j], {"gr": peer(j)})
        for j in range(1, n_gr)
    ]
    own_o = pltpu.make_async_copy(ob.at[r], out_o.at[:, cols(r)], loc.at[5])
    own_o.start()
    br[:, cols(r)] = bq[r]
    for m in range(n_gc - 1, -1, -1):
        if not any(m & bit for bit in firsts):
            grad_rows(m)
    later = [
        sorted((m for m in range(1, n_gc) if not m & firsts[h]), key=lambda m: -rank(h, m))
        for h in range(2)
    ]
    for pair in zip(*later):
        for h, m in enumerate(pair):
            bit = next(bit for bit in sides[h] if m & bit)
            push(h, m, bit, gathered(h, m))
    for copy in k_all:
        copy.wait_recv()
    local_all.wait()
    step = 256

    def input_rows(i):
        iv[:, i * step:(i + 1) * step] = lax.dot_general(
            br[...], wv[i * step:(i + 1) * step, :], (((1,), (1,)), ((), ())),
            preferred_element_type=f32,
        )
    steps = width // step
    for i in range(steps // 2):
        input_rows(i)
    for h in range(2):
        wa[r, :, h * part:(h + 1) * part] = (gathered(h, 0) * scale).astype(bf16)
    w_far = [send(wa.at[r], wa.at[r], w_s.at[d], w_r.at[d], {"gr": ahead(d)}) for d in far]
    w_mate = send(wa.at[r], wa.at[r], w_s.at[0], w_r.at[0], {"gr": mate})
    w_out = []

    def keep(s, j):
        w_out.append(pltpu.make_async_copy(wa.at[s], wg_o.at[:, cols(s)], loc.at[7 + j]))
        w_out[-1].start()

    keep(r, 0)
    for i in range(steps // 2, steps):
        input_rows(i)
    own_i = pltpu.make_async_copy(iv, ig_o, loc.at[6])
    own_i.start()
    w_next = []
    for d in far:
        w_far[d - 1].wait_recv()
        s = behind(d)
        w_next.append(send(wa.at[s], wa.at[s], v_s.at[d], v_r.at[d], {"gr": mate}))
        keep(s, 2 * d)
    w_mate.wait_recv()
    keep(mate, 1)
    for d in far:
        w_next[d - 1].wait_recv()
        keep(behind(d) + 1 - 2 * core, 2 * d + 1)
    for copy in [f_mate, a_mate, w_mate] + a_far + a_next + w_far + w_next + c_all + k_all:
        copy.wait_send()
    for group in (f_far, f_next, x_all):
        for copy in group.values():
            copy.wait_send()
    for copy in o_all:
        copy.wait()
    for copy in w_out:
        copy.wait()
    own_o.wait()
    own_i.wait()


def finish_kernel(out_b, ig, wg_b, out_o, ig_o, wg_o, ov, iv, wv, of, wf, sem):
    loads = [
        pltpu.make_async_copy(src, dst, sem.at[i])
        for i, (src, dst) in enumerate(((ig, iv), (out_b, ov), (wg_b, wv)))
    ]
    stores = [
        pltpu.make_async_copy(src, dst, sem.at[3 + i])
        for i, (src, dst) in enumerate(((iv, ig_o), (of, out_o), (wf, wg_o)))
    ]
    for copy in loads:
        copy.start()
    loads[0].wait()
    stores[0].start()
    loads[1].wait()
    of[...] = ov[...].astype(jnp.float32)
    stores[1].start()
    loads[2].wait()
    wf[...] = wv[...].astype(jnp.float32)
    stores[2].start()
    for copy in stores:
        copy.wait()


def by_columns(features, weight, cotangent, block_values, block_codes, block_count):
    n_gr, n_gc = lax.axis_size("gr"), lax.axis_size("gc")
    rows, width = features.shape
    slots = block_values.shape[1]
    share, depth = width // n_gr, width // n_gc
    f32, bf16 = jnp.float32, jnp.bfloat16
    dma = pltpu.SemaphoreType.DMA
    everywhere = pl.BlockSpec(memory_space=pl.ANY)
    outside = pl.BlockSpec(memory_space=pltpu.HBM)
    scalars = pl.BlockSpec(memory_space=pltpu.SMEM)
    chips = n_gr // 2
    out, input_grad, weight_grad = pl.pallas_call(
        functools.partial(layer_kernel, n_gr, n_gc, (rows * n_gr * n_gc) ** (-0.5)),
        out_shape=(
            jax.ShapeDtypeStruct((rows, width), bf16),
            jax.ShapeDtypeStruct((rows, width), f32),
            jax.ShapeDtypeStruct((depth, width), bf16),
        ),
        in_specs=[outside] * 4 + [scalars] * 2,
        out_specs=(everywhere,) * 3,
        scratch_shapes=[
            pltpu.VMEM((n_gr, rows, width), bf16),
            pltpu.VMEM((width, n_gr * rows), bf16),
            pltpu.VMEM((width, share), bf16),
            pltpu.VMEM((width, width), bf16),
            pltpu.VMEM((slots, rows, rows), bf16),
            pltpu.VMEM((n_gr * rows, n_gr * rows), bf16),
            pltpu.VMEM((n_gr * rows, share), bf16),
            pltpu.VMEM((n_gr, rows, share), bf16),
            pltpu.VMEM((n_gr, rows, share), f32),
            pltpu.VMEM((n_gr, rows, share), bf16),
            pltpu.VMEM((n_gr, rows, share), bf16),
            pltpu.VMEM((rows, width), bf16),
            pltpu.VMEM((rows, width), f32),
            pltpu.VMEM((2, n_gc, depth, share // 2), bf16),
            pltpu.VMEM((2, n_gc, depth, share // 2), bf16),
            pltpu.VMEM((n_gc, depth, share), f32),
            pltpu.VMEM((n_gr, depth, share), bf16),
            dma((7 + n_gr,)),
        ]
        + [dma((chips, 2))] * 4
        + [dma((chips,))] * 8
        + [dma((n_gr,))] * 6
        + [dma((2, n_gc))] * 2,
        compiler_params=pltpu.CompilerParams(
            collective_id=0, has_side_effects=True, vmem_limit_bytes=GRANT
        ),
        cost_estimate=pl.CostEstimate(
            flops=2 * rows * width * (3 * width + 2 * n_gr * rows),
            bytes_accessed=6 * width * width,
            transcendentals=rows * width,
        ),
    )(features, weight, cotangent, block_values, block_codes, block_count)
    return pl.pallas_call(
        finish_kernel,
        out_shape=(
            jax.ShapeDtypeStruct((rows, width), f32),
            jax.ShapeDtypeStruct((rows, width), f32),
            jax.ShapeDtypeStruct((depth, width), f32),
        ),
        in_specs=[everywhere] * 3,
        out_specs=(everywhere,) * 3,
        scratch_shapes=[
            pltpu.VMEM((rows, width), bf16),
            pltpu.VMEM((rows, width), f32),
            pltpu.VMEM((depth, width), bf16),
            pltpu.VMEM((rows, width), f32),
            pltpu.VMEM((depth, width), f32),
            dma((6,)),
        ],
        compiler_params=pltpu.CompilerParams(vmem_limit_bytes=GRANT),
    )(out, input_grad, weight_grad)


def local(features, weight, cotangent, block_values, block_codes, block_count):
    n_gr, n_gc = lax.axis_size("gr"), lax.axis_size("gc")
    rows, width = features.shape
    whole = width % (256 * n_gr) == 0 and width % (16 * n_gc) == 0
    even = n_gr % 2 == 0 and n_gc in (4, 8, 16, 32)
    take = by_columns if whole and even and rows == block_values.shape[-1] else by_rows
    return take(features, weight, cotangent, block_values, block_codes, block_count)


def solution(mesh):
    in_specs = (
        P(("gr", "gc"), None),
        P(),
        P(("gr", "gc"), None),
        P(("gr", "gc"), None, None, None),
        P(("gr", "gc"), None),
        P(("gr", "gc")),
    )
    out_specs = (P(("gr", "gc"), None), P(("gr", "gc"), None), P("gc", None))
    return jax.shard_map(local, mesh=mesh, in_specs=in_specs, out_specs=out_specs, check_vma=False)
```

profile of v0, /device:TPU:1, one launch (start us, length us, event | category | flops | bytes accessed | tf_op | source)
XLA Modules:
  0.0 37.3 jit_solution(14036052776141654403)
XLA Ops:
  1.3 33.8 %shard_map.85 = (bf16[128,1024]{1,0:T(8,128)(2,1)}, f32[128,1024]{1,0:T(8,128)}, bf16[128,1024]{1,0:T(8,128)(2,1)}) custom-call(bf16[128,1024]{1,0:T(8,128)(2,1)} %feat.1, bf16[1024,1024]{1,0:T(8,128)(2,1)} %wt.1, bf16[128,1024]{1,0:T(8,128)(2,1)} %cot.1, bf16[1,4,128,128]{3,2,1,0:T(8,128)(2,1)} %vals.1, s32[1,4]{1,0:T(1,128)} %codes.1, s32[1]{0:T(128)S(6)} %copy.9.count), custom_call_target="tpu_custom_call" | custom-call | flops 1073741824 | bytes 6291456 | tf_op jit(solution)/shard_map/pallas_call | solution.py:371
  35.1 2.2 %shard_map.86 = (f32[128,1024]{1,0:T(8,128)}, f32[128,1024]{1,0:T(8,128)}, f32[128,1024]{1,0:T(8,128)}) custom-call(bf16[128,1024]{1,0:T(8,128)(2,1)} %get-tuple-element.6.out_b, f32[128,1024]{1,0:T(8,128)} %get-tuple-element.7.ig, bf16[128,1024]{1,0:T(8,128)(2,1)} %get-tuple-element.8.wg_b), custom_call_target="tpu_custom_call" | custom-call | tf_op jit(solution)/shard_map/pallas_call | solution.py:413
where the time goes:
time: 37.5 us; the launch traced here: 37.3 us
  Pallas kernels  36 us (96%)
  between operations  1.29 us (3%)
    pallas_call x1, Pallas kernels, by_columns(): pl.pallas_call(functools.partial(layer_kernel, n_gr, n_gc, (rows * n_gr *...  33.8 us
    pallas_call x1, Pallas kernels, by_columns(): pl.pallas_call(finish_kernel, out_shape=(jax.ShapeDtypeStruct((rows, widt...  2.23 us

commit v1 on v0

--- a/solution.py
+++ b/solution.py
@@ -77,7 +77,7 @@
     n_gr, n_gc, scale,
     feat, wt, cot, vals, codes, count,
     out_o, ig_o, wg_o,
-    fa, ft, wq, wv, vv, aa, pj, cq, sl, ob, bq, br, iv, xs, xr, ac, wa,
+    fa, ft, wq, wv, vv, aa, pj, cq, sl, ob, px, oe, bq, br, iv, xs, xr, ac, wa,
     loc, f_s, f_r, g_s, g_r, a_s, a_r, b_s, b_r, w_s, w_r, v_s, v_r,
     c_s, c_r, o_s, o_r, k_s, k_r, x_s, x_r,
 ):
@@ -212,7 +212,7 @@
     for i in range(n_gr):
         summed = jnp.dot(aa[i * rows:(i + 1) * rows, :], pj[...], preferred_element_type=f32)
         sigmoid = jax.nn.sigmoid(summed)
-        ob[i] = (summed * sigmoid).astype(bf16)
+        ob[i] = summed * sigmoid
         sl[i] = sigmoid * (1.0 + summed * (1.0 - sigmoid))
     for d in far:
         turn(behind(d))
@@ -264,12 +264,9 @@
         send(bq.at[peer(j)], br.at[:, cols(r)], k_s.at[j], k_r.at[j], {"gr": peer(j)})
         for j in range(1, n_gr)
     ]
-    o_all = [
-        send(ob.at[peer(j)], out_o.at[:, cols(r)], o_s.at[j], o_r.at[j], {"gr": peer(j)})
-        for j in range(1, n_gr)
-    ]
-    own_o = pltpu.make_async_copy(ob.at[r], out_o.at[:, cols(r)], loc.at[5])
-    own_o.start()
+    o_all = [send(ob.at[mate], out_o.at[:, cols(r)], o_s.at[0], o_r.at[0], {"gr": mate})]
+    o_own = [pltpu.make_async_copy(ob.at[r], out_o.at[:, cols(r)], loc.at[5])]
+    o_own[0].start()
     br[:, cols(r)] = bq[r]
     for m in range(n_gc - 1, -1, -1):
         if not any(m & bit for bit in firsts):
@@ -278,13 +275,35 @@
         sorted((m for m in range(1, n_gc) if not m & firsts[h]), key=lambda m: -rank(h, m))
         for h in range(2)
     ]
-    for pair in zip(*later):
+
+    def other_outputs():
+        local_all.wait()
+        for d in far:
+            q = behind(d)
+            px[...] = jnp.dot(
+                fa[...].reshape(n_gr * rows, width), wv[:, cols(q)], preferred_element_type=f32
+            ).astype(bf16)
+            for side, s in enumerate((mate, r)):
+                summed = jnp.dot(aa[rowsof(s), :], px[...], preferred_element_type=f32)
+                oe[d, side] = summed * jax.nn.sigmoid(summed)
+            o_all.append(
+                send(oe.at[d, 0], out_o.at[:, cols(q)], o_s.at[d], o_r.at[d], {"gr": mate})
+            )
+            o_own.append(
+                pltpu.make_async_copy(oe.at[d, 1], out_o.at[:, cols(q)], loc.at[6 + n_gr + d])
+            )
+            o_own[-1].start()
+
+    for turn_of, pair in enumerate(zip(*later)):
+        if turn_of == 1:
+            other_outputs()
         for h, m in enumerate(pair):
             bit = next(bit for bit in sides[h] if m & bit)
             push(h, m, bit, gathered(h, m))
+    if len(later[0]) < 2:
+        other_outputs()
     for copy in k_all:
         copy.wait_recv()
-    local_all.wait()
     step = 256
 
     def input_rows(i):
@@ -330,25 +349,25 @@
         copy.wait()
     for copy in w_out:
         copy.wait()
-    own_o.wait()
+    for copy in o_own:
+        copy.wait()
     own_i.wait()
 
 
-def finish_kernel(out_b, ig, wg_b, out_o, ig_o, wg_o, ov, iv, wv, of, wf, sem):
+def finish_kernel(out_b, ig, wg_b, out_o, ig_o, wg_o, ov, iv, wv, wf, sem):
     loads = [
         pltpu.make_async_copy(src, dst, sem.at[i])
         for i, (src, dst) in enumerate(((ig, iv), (out_b, ov), (wg_b, wv)))
     ]
     stores = [
         pltpu.make_async_copy(src, dst, sem.at[3 + i])
-        for i, (src, dst) in enumerate(((iv, ig_o), (of, out_o), (wf, wg_o)))
+        for i, (src, dst) in enumerate(((iv, ig_o), (ov, out_o), (wf, wg_o)))
     ]
     for copy in loads:
         copy.start()
     loads[0].wait()
     stores[0].start()
     loads[1].wait()
-    of[...] = ov[...].astype(jnp.float32)
     stores[1].start()
     loads[2].wait()
     wf[...] = wv[...].astype(jnp.float32)
@@ -371,7 +390,7 @@
     out, input_grad, weight_grad = pl.pallas_call(
         functools.partial(layer_kernel, n_gr, n_gc, (rows * n_gr * n_gc) ** (-0.5)),
         out_shape=(
-            jax.ShapeDtypeStruct((rows, width), bf16),
+            jax.ShapeDtypeStruct((rows, width), f32),
             jax.ShapeDtypeStruct((rows, width), f32),
             jax.ShapeDtypeStruct((depth, width), bf16),
         ),
@@ -387,7 +406,9 @@
             pltpu.VMEM((n_gr * rows, share), bf16),
             pltpu.VMEM((n_gr, rows, share), bf16),
             pltpu.VMEM((n_gr, rows, share), f32),
-            pltpu.VMEM((n_gr, rows, share), bf16),
+            pltpu.VMEM((n_gr, rows, share), f32),
+            pltpu.VMEM((n_gr * rows, share), bf16),
+            pltpu.VMEM((chips, 2, rows, share), f32),
             pltpu.VMEM((n_gr, rows, share), bf16),
             pltpu.VMEM((rows, width), bf16),
             pltpu.VMEM((rows, width), f32),
@@ -395,7 +416,7 @@
             pltpu.VMEM((2, n_gc, depth, share // 2), bf16),
             pltpu.VMEM((n_gc, depth, share), f32),
             pltpu.VMEM((n_gr, depth, share), bf16),
-            dma((7 + n_gr,)),
+            dma((6 + n_gr + chips,)),
         ]
         + [dma((chips, 2))] * 4
         + [dma((chips,))] * 8
@@ -420,10 +441,9 @@
         in_specs=[everywhere] * 3,
         out_specs=(everywhere,) * 3,
         scratch_shapes=[
-            pltpu.VMEM((rows, width), bf16),
+            pltpu.VMEM((rows, width), f32),
             pltpu.VMEM((rows, width), f32),
             pltpu.VMEM((depth, width), bf16),
-            pltpu.VMEM((rows, width), f32),
             pltpu.VMEM((depth, width), f32),
             dma((6,)),
         ],

time: 37.5 us -> 37.4 us (level)
  no operation moved by 1% of the time
where the time goes in v1:
time: 37.4 us; the launch traced here: 37.2 us
  Pallas kernels  35.9 us (96%)
  between operations  1.29 us (3%)
    pallas_call x1, Pallas kernels, by_columns(): pl.pallas_call(functools.partial(layer_kernel, n_gr, n_gc, (rows * n_gr *...  33.7 us
    pallas_call x1, Pallas kernels, by_columns(): pl.pallas_call(finish_kernel, out_shape=(jax.ShapeDtypeStruct((rows, widt...  2.23 us

profile of v1, /device:TPU:1, one launch (start us, length us, event | category | flops | bytes accessed | tf_op | source)
XLA Modules:
  0.0 37.2 jit_solution(4051630755294341664)
XLA Ops:
  1.3 33.7 %shard_map.85 = (f32[128,1024]{1,0:T(8,128)}, f32[128,1024]{1,0:T(8,128)}, bf16[128,1024]{1,0:T(8,128)(2,1)}) custom-call(bf16[128,1024]{1,0:T(8,128)(2,1)} %feat.1, bf16[1024,1024]{1,0:T(8,128)(2,1)} %wt.1, bf16[128,1024]{1,0:T(8,128)(2,1)} %cot.1, bf16[1,4,128,128]{3,2,1,0:T(8,128)(2,1)} %vals.1, s32[1,4]{1,0:T(1,128)} %codes.1, s32[1]{0:T(128)S(6)} %copy.9.count), custom_call_target="tpu_custom_call" | custom-call | flops 1073741824 | bytes 6291456 | tf_op jit(solution)/shard_map/pallas_call | solution.py:390
  35.0 2.2 %shard_map.86 = (f32[128,1024]{1,0:T(8,128)}, f32[128,1024]{1,0:T(8,128)}, f32[128,1024]{1,0:T(8,128)}) custom-call(f32[128,1024]{1,0:T(8,128)} %get-tuple-element.6.out_b, f32[128,1024]{1,0:T(8,128)} %get-tuple-element.7.ig, bf16[128,1024]{1,0:T(8,128)(2,1)} %get-tuple-element.8.wg_b), custom_call_target="tpu_custom_call" | custom-call | tf_op jit(solution)/shard_map/pallas_call | solution.py:434

commit v2 on v1

--- a/solution.py
+++ b/solution.py
@@ -167,6 +167,13 @@
     def project(s):
         pj[rowsof(s), :] = jnp.dot(fa[s], wq[...], preferred_element_type=f32).astype(bf16)
 
+    def project_other(d, c):
+        at = pl.ds(pl.multiple_of(c * 2 * rows, 2 * rows), 2 * rows)
+        px[d, at, :] = jnp.dot(
+            fa[pl.ds(c * 2, 2)].reshape(2 * rows, width), wv[:, cols(behind(d))],
+            preferred_element_type=f32,
+        ).astype(bf16)
+
     def turn(s):
         ft[:, rowsof(s)] = fa[s].T
 
@@ -177,6 +184,9 @@
     f_mate.wait_recv()
     project(mate)
     turn(mate)
+    local_all.wait()
+    for d in far:
+        project_other(d, chip)
 
     f_next = {}
     c_all = []
@@ -209,8 +219,9 @@
     for copy in a_next:
         copy.wait_recv()
 
+    sl[...] = jnp.dot(aa[...], pj[...], preferred_element_type=f32).reshape(sl.shape)
     for i in range(n_gr):
-        summed = jnp.dot(aa[i * rows:(i + 1) * rows, :], pj[...], preferred_element_type=f32)
+        summed = sl[i]
         sigmoid = jax.nn.sigmoid(summed)
         ob[i] = summed * sigmoid
         sl[i] = sigmoid * (1.0 + summed * (1.0 - sigmoid))
@@ -221,11 +232,8 @@
     for copy in c_all:
         copy.wait_recv()
     slope_all = (cq[...].astype(f32) * sl[...]).astype(bf16).reshape(n_gr * rows, share)
-    for i in range(n_gr):
-        bq[i] = jnp.dot(
-            aa[i * rows:(i + 1) * rows, :], slope_all, preferred_element_type=f32
-        ).astype(bf16)
-    back = bq[...].reshape(n_gr * rows, share)
+    back = jnp.dot(aa[...], slope_all, preferred_element_type=f32).astype(bf16)
+    bq[...] = back.reshape(bq.shape)
 
     depth, part = width // n_gc, share // 2
     sides = [bits, bits[1::-1] + bits[2:]]
@@ -237,12 +245,19 @@
             xs.at[h, m], xr.at[h, m], x_s.at[h, m], x_r.at[h, m], {"gc": flip(g, bit)}
         )
 
-    def grad_rows(m):
+    def grad_rows(top):
+        at = flip(g, top) // bits[-1] * bits[-1] * depth
+        at = pl.ds(pl.multiple_of(at, bits[-1] * depth), bits[-1] * depth)
+        ac[at, :] = jnp.dot(
+            ft[at, :], bq[...].reshape(n_gr * rows, share), preferred_element_type=f32
+        )
+
+    def own_part(h, m):
         at = pl.ds(pl.multiple_of(flip(g, m) * depth, depth), depth)
-        ac[m] = jnp.dot(ft[at, :], back, preferred_element_type=f32)
+        return ac[at, h * part:(h + 1) * part]
 
     def gathered(h, m):
-        total = ac[m, :, h * part:(h + 1) * part]
+        total = own_part(h, m)
         for bit in sides[h]:
             if m & bit:
                 break
@@ -254,12 +269,12 @@
         return sum(1 << t for t, bit in enumerate(sides[h]) if m & bit)
 
     firsts = [order[0] for order in sides]
-    for m in range(n_gc - 1, 0, -1):
-        if any(m & bit for bit in firsts):
-            grad_rows(m)
+    for top in (bits[-1], 0):
+        grad_rows(top)
+        for m in range(top + bits[-1] - 1, max(top - 1, 0), -1):
             for h, bit in enumerate(firsts):
                 if m & bit:
-                    push(h, m, bit, ac[m, :, h * part:(h + 1) * part])
+                    push(h, m, bit, own_part(h, m))
     k_all = [
         send(bq.at[peer(j)], br.at[:, cols(r)], k_s.at[j], k_r.at[j], {"gr": peer(j)})
         for j in range(1, n_gr)
@@ -268,23 +283,18 @@
     o_own = [pltpu.make_async_copy(ob.at[r], out_o.at[:, cols(r)], loc.at[5])]
     o_own[0].start()
     br[:, cols(r)] = bq[r]
-    for m in range(n_gc - 1, -1, -1):
-        if not any(m & bit for bit in firsts):
-            grad_rows(m)
     later = [
         sorted((m for m in range(1, n_gc) if not m & firsts[h]), key=lambda m: -rank(h, m))
         for h in range(2)
     ]
 
     def other_outputs():
-        local_all.wait()
         for d in far:
             q = behind(d)
-            px[...] = jnp.dot(
-                fa[...].reshape(n_gr * rows, width), wv[:, cols(q)], preferred_element_type=f32
-            ).astype(bf16)
+            for e in far:
+                project_other(d, lax.rem(chip + e, chips))
             for side, s in enumerate((mate, r)):
-                summed = jnp.dot(aa[rowsof(s), :], px[...], preferred_element_type=f32)
+                summed = jnp.dot(aa[rowsof(s), :], px[d], preferred_element_type=f32)
                 oe[d, side] = summed * jax.nn.sigmoid(summed)
             o_all.append(
                 send(oe.at[d, 0], out_o.at[:, cols(q)], o_s.at[d], o_r.at[d], {"gr": mate})
@@ -407,14 +417,14 @@
             pltpu.VMEM((n_gr, rows, share), bf16),
             pltpu.VMEM((n_gr, rows, share), f32),
             pltpu.VMEM((n_gr, rows, share), f32),
-            pltpu.VMEM((n_gr * rows, share), bf16),
+            pltpu.VMEM((chips, n_gr * rows, share), bf16),
             pltpu.VMEM((chips, 2, rows, share), f32),
             pltpu.VMEM((n_gr, rows, share), bf16),
             pltpu.VMEM((rows, width), bf16),
             pltpu.VMEM((rows, width), f32),
             pltpu.VMEM((2, n_gc, depth, share // 2), bf16),
             pltpu.VMEM((2, n_gc, depth, share // 2), bf16),
-            pltpu.VMEM((n_gc, depth, share), f32),
+            pltpu.VMEM((n_gc * depth, share), f32),
             pltpu.VMEM((n_gr, depth, share), bf16),
             dma((6 + n_gr + chips,)),
         ]

time: 37.4 us -> 37.6 us (level)
  no operation moved by 1% of the time
where the time goes in v2:
time: 37.6 us; the launch traced here: 37.5 us
  Pallas kernels  36.2 us (96%)
  between operations  1.29 us (3%)
    pallas_call x1, Pallas kernels, by_columns(): pl.pallas_call(functools.partial(layer_kernel, n_gr, n_gc, (rows * n_gr *...  34 us
    pallas_call x1, Pallas kernels, by_columns(): pl.pallas_call(finish_kernel, out_shape=(jax.ShapeDtypeStruct((rows, widt...  2.23 us

profile of v2, /device:TPU:1, one launch (start us, length us, event | category | flops | bytes accessed | tf_op | source)
XLA Modules:
  0.0 37.5 jit_solution(2545062076104203193)
XLA Ops:
  1.3 34.0 %shard_map.85 = (f32[128,1024]{1,0:T(8,128)}, f32[128,1024]{1,0:T(8,128)}, bf16[128,1024]{1,0:T(8,128)(2,1)}) custom-call(bf16[128,1024]{1,0:T(8,128)(2,1)} %feat.1, bf16[1024,1024]{1,0:T(8,128)(2,1)} %wt.1, bf16[128,1024]{1,0:T(8,128)(2,1)} %cot.1, bf16[1,4,128,128]{3,2,1,0:T(8,128)(2,1)} %vals.1, s32[1,4]{1,0:T(1,128)} %codes.1, s32[1]{0:T(128)S(6)} %copy.9.count), custom_call_target="tpu_custom_call" | custom-call | flops 1073741824 | bytes 6291456 | tf_op jit(solution)/shard_map/pallas_call | solution.py:400
  35.2 2.2 %shard_map.86 = (f32[128,1024]{1,0:T(8,128)}, f32[128,1024]{1,0:T(8,128)}, f32[128,1024]{1,0:T(8,128)}) custom-call(f32[128,1024]{1,0:T(8,128)} %get-tuple-element.6.out_b, f32[128,1024]{1,0:T(8,128)} %get-tuple-element.7.ig, bf16[128,1024]{1,0:T(8,128)(2,1)} %get-tuple-element.8.wg_b), custom_call_target="tpu_custom_call" | custom-call | tf_op jit(solution)/shard_map/pallas_call | solution.py:444
